TPU v7x, 512 devices: a whole 4x8x8 slice. The times are simulated.
512 devices in a mesh: occ: 16 (over y, core), vir: 32 (over x, z).
Axes of the slice: x: 4, y: 8, z: 8, core: 2. Of those that a mesh axis runs over, the one named last changes fastest.
Arguments:
- amplitudes: float32 [2048, 12288], P('occ', 'vir'), may hold values from -6 to 6
- integrals: float32 [12288, 4096], P('vir', 'occ'), may hold values from -0.109375 to 0.109375
- pair_mask: int32 [32, 192], P('occ', 'vir'), may hold values 0 or 1
- tile_mask: int32 [192, 64], P('vir', 'occ'), may hold values 0 or 1
Outputs:
- residual: float32 [2048, 4096], P('occ', 'vir')
Inputs may be any that keep to these rules, and one draw needn't show every extreme that they name: `pair_mask`: 0 marks a tile that is absent and contributes nothing. `tile_mask`: 0 marks a tile that is absent and contributes nothing.
All inputs are finite; a program needn't handle non-finite values. No bound on the sum of `pair_mask` or of `tile_mask` on one device may be relied on, other than what follows from the above.
Results may differ from a plain program's by a relative error of at most 0.00007.
Values sent between devices are 32-bit elements; how exact they have to be, the bound alone decides.
No kernel may reach another device: no remote copies, remote signals or barrier semaphores. Data moves between devices by JAX's collectives and lax.ppermute only.
A program may use at most 64 MiB of HBM per device.

v0:
```python
import jax
import jax.numpy as jnp
from jax import lax
from jax.sharding import Mesh, PartitionSpec as P


def expand(mask, width):
    grown = jnp.repeat(mask.astype(jnp.float32), width, axis=0)
    return jnp.repeat(grown, width, axis=1)


def body(amplitudes, integrals, pair_mask, tile_mask):
    tile_width = amplitudes.shape[1] // pair_mask.shape[1]
    masked_v = integrals * expand(tile_mask, tile_width)
    other_v = lax.ppermute(masked_v, "l", [(0, 1), (1, 0)])
    masked_t = amplitudes * expand(pair_mask, tile_width)
    rows = lax.all_gather(masked_t, "h", axis=0, tiled=True)
    near = lax.all_gather(masked_v, "c", axis=1, tiled=True)
    far = lax.all_gather(other_v, "c", axis=1, tiled=True)
    low = lax.axis_index("l") == 0
    columns = jnp.concatenate([jnp.where(low, near, far), jnp.where(low, far, near)], axis=1)
    partial_sum = jnp.dot(
        rows, columns, precision=lax.Precision.HIGH, preferred_element_type=jnp.float32
    )
    count = lax.axis_size("x")
    parts = lax.all_to_all(partial_sum, "x", 0, 0, tiled=True)
    over_x = parts.reshape(count, -1, parts.shape[1]).sum(0)
    depth = lax.axis_size("z")
    pieces = over_x.reshape(over_x.shape[0], depth, -1).transpose(1, 0, 2)
    pieces = lax.all_to_all(pieces, "z", 0, 0, tiled=True)
    total = pieces.sum(0)
    swap = [(h * count + x, x * count + h) for h in range(count) for x in range(count)]
    return lax.ppermute(total, ("h", "x"), swap)


def solution(mesh):
    fine = Mesh(mesh.devices.reshape(4, 2, 2, 4, 8), ("h", "l", "c", "x", "z"))
    occ, vir = (("h", "l", "c"), ("x", "z"))
    in_specs = (P(occ, vir), P(vir, occ), P(occ, vir), P(vir, occ))
    return jax.shard_map(body, mesh=fine, in_specs=in_specs, out_specs=P(occ, vir), check_vma=False)
```

profile of v0, /device:TPU:4, one launch (start us, length us, event | category | flops | bytes accessed | tf_op | source)
XLA Modules:
  0.0 106.9 jit_solution(17523145308158582603)
XLA Ops:
  0.0 0.0 copy-start.1
  0.0 0.0 copy-start
  0.0 0.7 convert_element_type.7
  0.7 0.1 broadcast_in_dim.14
  0.8 0.1 reshape.21
  0.9 1.2 %copy.21 = f32[384,256]{0,1:T(8,128)S(1)} copy(f32[384,256]{1,0:T(8,128)} %param.5) | data formatting | bytes 786432 | tf_op args[1]
  2.1 3.5 %collective-permute-start = (f32[384,256]{0,1:T(8,128)S(1)}, f32[384,256]{0,1:T(8,128)S(1)}, u32[]{:S(2)}, u32[]{:S(2)}) collective-permute-start(f32[384,256]{0,1:T(8,128)S(1)} %bitcast_multiply_fusion), channel_id=1, source_target_pairs={{0,64},{64,0},{1,65},{65,1},{2,66},{66,2},{3,67},{67,3},{4,68},{68... | collective-permute-start | bytes 1179656 | tf_op jit(solution)/shard_map/ppermute | solution.py:15
  5.6 2.4 %all_gather.10 = f32[384,512]{0,1:T(8,128)S(1)} all-gather(f32[384,256]{0,1:T(8,128)S(1)} %bitcast_multiply_fusion), channel_id=1, replica_groups=mesh['h'=4,'l'=2,'c'=2,'x'=4,'z'=8] {'c'}, dimensions={1}, use_global_device_ids=true | all-gather | bytes 1179648 | tf_op jit(solution)/shard_map/all_gather | solution.py:18
  7.9 0.0 copy-done.1
  8.0 0.1 copy.19
  8.1 0.1 broadcast_in_dim.12
  8.1 0.1 reshape.19
  8.2 0.0 copy-done
  8.2 0.1 copy.20
  8.4 24.4 %all_gather.9 = f32[512,384]{0,1:T(8,128)S(1)} all-gather(f32[128,384]{0,1:T(8,128)S(1)} %bitcast_multiply_fusion.1), channel_id=1, replica_groups=mesh['h'=4,'l'=2,'c'=2,'x'=4,'z'=8] {'h'}, dimensions={0}, use_global_device_ids=true | all-gather | bytes 983040 | tf_op jit(solution)/shard_map/all_gather | solution.py:17
  32.8 0.0 collective-permute-done
  32.8 2.4 %all_gather.11 = f32[384,512]{0,1:T(8,128)S(1)} all-gather(f32[384,256]{0,1:T(8,128)S(1)} %collective-permute-done), channel_id=1, replica_groups=mesh['h'=4,'l'=2,'c'=2,'x'=4,'z'=8] {'c'}, dimensions={1}, use_global_device_ids=true | all-gather | bytes 1179648 | tf_op jit(solution)/shard_map/all_gather | solution.py:19
  35.2 0.1 broadcast_select_fusion.1
  35.3 2.8 %fusion = f32[512,1024]{1,0:T(8,128)S(1)} fusion(f32[512,384]{0,1:T(8,128)S(1)} %all_gather.9, f32[384,512]{0,1:T(8,128)S(1)} %get-tuple-element.6, f32[384,512]{0,1:T(8,128)S(1)} %get-tuple-element.5), kind=kOutput, calls=%fused_computation | convolution fusion | flops 1208352768 | bytes 4456448 | tf_op jit(solution)/shard_map/dot_general | solution.py:22
  38.1 28.5 %all_to_all.14 = f32[4,128,1024]{2,1,0:T(8,128)S(1)} all-to-all(f32[4,128,1024]{2,1,0:T(8,128)S(1)} %bitcast.13), channel_id=1, replica_groups=mesh['h'=4,'l'=2,'c'=2,'x'=4,'z'=8] {'x'}, dimensions={0} | all-to-all | bytes 4194304 | tf_op jit(solution)/shard_map/all_to_all | solution.py:26
  66.6 0.2 reduce_sum.18
  66.8 0.2 copy.22
  67.0 0.2 copy.23
  67.2 26.5 %all_to_all.15 = f32[8,128,128]{2,1,0:T(8,128)S(1)} all-to-all(f32[8,128,128]{2,1,0:T(8,128)S(1)} %copy.23), channel_id=1, replica_groups=mesh['h'=4,'l'=2,'c'=2,'x'=4,'z'=8] {'z'}, dimensions={0} | all-to-all | bytes 1048576 | tf_op jit(solution)/shard_map/all_to_all | solution.py:30
  93.8 6.3 %collective-permute-start.1 = (f32[128,128]{1,0:T(8,128)S(1)}, f32[128,128]{1,0:T(8,128)S(1)}, u32[]{:S(2)}, u32[]{:S(2)}) collective-permute-start(f32[128,128]{1,0:T(8,128)S(1)} %reduce_sum.19), channel_id=1, source_target_pairs={{0,0},{8,128},{16,256},{24,384},{128,8},{136,136},{144,264},{152,3... | collective-permute-start | bytes 196616 | tf_op jit(solution)/shard_map/ppermute | solution.py:33
  100.0 6.2 %collective-permute-done.1 = f32[128,128]{1,0:T(8,128)S(1)} collective-permute-done((f32[128,128]{1,0:T(8,128)S(1)}, f32[128,128]{1,0:T(8,128)S(1)}, u32[]{:S(2)}, u32[]{:S(2)}) %collective-permute-start.1) | collective-permute-done | bytes 65568 | tf_op jit(solution)/shard_map/ppermute | solution.py:33
  106.2 0.6 copy.25
  (4 shorter events, 0.1 us)
Async XLA Ops:
  0.0 8.0 %copy-start.1 = (s32[2,6]{1,0:T(2,128)S(1)}, s32[2,6]{1,0:T(2,128)}, u32[]{:S(2)}) copy-start(s32[2,6]{1,0:T(2,128)} %param.6) | copy-start | bytes 148
  0.0 8.2 %copy-start = (f32[128,384]{1,0:T(8,128)S(1)}, f32[128,384]{1,0:T(8,128)}, u32[]{:S(2)}) copy-start(f32[128,384]{1,0:T(8,128)} %param.4) | copy-start | bytes 589828
  2.1 30.7 %collective-permute-start = (f32[384,256]{0,1:T(8,128)S(1)}, f32[384,256]{0,1:T(8,128)S(1)}, u32[]{:S(2)}, u32[]{:S(2)}) collective-permute-start(f32[384,256]{0,1:T(8,128)S(1)} %bitcast_multiply_fusion), channel_id=1, source_target_pairs={{0,64},{64,0},{1,65},{65,1},{2,66},{66,2},{3,67},{67,3},{4,68},{68... | collective-permute-start | bytes 1179656 | tf_op jit(solution)/shard_map/ppermute | solution.py:15
  93.8 12.5 %collective-permute-start.1 = (f32[128,128]{1,0:T(8,128)S(1)}, f32[128,128]{1,0:T(8,128)S(1)}, u32[]{:S(2)}, u32[]{:S(2)}) collective-permute-start(f32[128,128]{1,0:T(8,128)S(1)} %reduce_sum.19), channel_id=1, source_target_pairs={{0,0},{8,128},{16,256},{24,384},{128,8},{136,136},{144,264},{152,3... | collective-permute-start | bytes 196616 | tf_op jit(solution)/shard_map/ppermute | solution.py:33
where the time goes:
time: 107 us
  blocking collectives  84.2 us (79%)
  starting transfers between devices  9.76 us (9%)
  waiting for transfers between devices  6.19 us (6%)
  matrix products  2.78 us (3%)
  local copies, waits for them, and re-layouts  2.71 us (3%)
  other arithmetic  1.09 us (1%)
    all_to_all x1, blocking collectives, body(): parts = lax.all_to_all(partial_sum, 'x', 0, 0, tiled=True)  28.5 us
    all_to_all x1, blocking collectives, body(): pieces = lax.all_to_all(pieces, 'z', 0, 0, tiled=True)  26.5 us
    all_gather x1, blocking collectives, body(): rows = lax.all_gather(masked_t, 'h', axis=0, tiled=True)  24.4 us
    ppermute x1, starting transfers between devices, body(): return lax.ppermute(total, ('h', 'x'), swap)  6.28 us
    ppermute x1, waiting for transfers between devices, body(): return lax.ppermute(total, ('h', 'x'), swap)  6.19 us
    ppermute x1, starting transfers between devices, body(): other_v = lax.ppermute(masked_v, 'l', [(0, 1), (1, 0)])  3.48 us
    dot_general x1, matrix products, body(): jnp.dot(rows, columns, precision=lax.Precision.HIGH, preferred_element_ty...  2.78 us
    all_gather x1, blocking collectives, body(): near = lax.all_gather(masked_v, 'c', axis=1, tiled=True)  2.37 us
  transfers between devices with their start and end apart: 2, of which 1 were waited for; matrix products, arithmetic and copies ran while one was open for 0% of the time, Pallas kernels for 0%

commit v1 on v0

--- a/solution.py
+++ b/solution.py
@@ -15,8 +15,11 @@
     other_v = lax.ppermute(masked_v, "l", [(0, 1), (1, 0)])
     masked_t = amplitudes * expand(pair_mask, tile_width)
     rows = lax.all_gather(masked_t, "h", axis=0, tiled=True)
-    near = lax.all_gather(masked_v, "c", axis=1, tiled=True)
-    far = lax.all_gather(other_v, "c", axis=1, tiled=True)
+    near, far = jnp.split(
+        lax.all_gather(jnp.concatenate([masked_v, other_v], 0), "c", axis=1, tiled=True),
+        [masked_v.shape[0]],
+        0,
+    )
     low = lax.axis_index("l") == 0
     columns = jnp.concatenate([jnp.where(low, near, far), jnp.where(low, far, near)], axis=1)
     partial_sum = jnp.dot(

time: 107 us -> 125 us (1.17)
  the two profiles are of different devices: /device:TPU:4 before, /device:TPU:40 now
where the time goes in v1:
time: 125 us; the launch traced here: 124 us
  blocking collectives  72.9 us (58%)
  waiting for transfers between devices  23.8 us (19%)
  between operations  13.5 us (11%)
  starting transfers between devices  5.4 us (4%)
  other arithmetic  3.37 us (3%)
  matrix products  2.77 us (2%)
  local copies, waits for them, and re-layouts  2.72 us (2%)
    all_to_all x1, blocking collectives, body(): parts = lax.all_to_all(partial_sum, 'x', 0, 0, tiled=True)  30.8 us
    all_to_all x1, blocking collectives, body(): pieces = lax.all_to_all(pieces, 'z', 0, 0, tiled=True)  24 us
    all_gather x1, blocking collectives, body(): rows = lax.all_gather(masked_t, 'h', axis=0, tiled=True)  18 us
    ppermute x1, waiting for transfers between devices, body(): return lax.ppermute(total, ('h', 'x'), swap)  10.4 us
    ppermute x1, waiting for transfers between devices, body(): other_v = lax.ppermute(masked_v, 'l', [(0, 1), (1, 0)])  9.48 us
    all_gather x1, waiting for transfers between devices, body(): lax.all_gather(jnp.concatenate([masked_v, other_v], 0), 'c', axis=1, tile...  3.84 us
    ppermute x1, starting transfers between devices, body(): other_v = lax.ppermute(masked_v, 'l', [(0, 1), (1, 0)])  3.39 us
    dot_general x1, matrix products, body(): jnp.dot(rows, columns, precision=lax.Precision.HIGH, preferred_element_ty...  2.77 us
  transfers between devices with their start and end apart: 3, of which 3 were waited for; matrix products, arithmetic and copies ran while one was open for 0% of the time, Pallas kernels for 0%

profile of v1, /device:TPU:40, one launch (start us, length us, event | category | flops | bytes accessed | tf_op | source)
XLA Modules:
  0.0 124.4 jit_solution(16396492333823880271)
XLA Ops:
  6.5 0.0 all-gather.2.cloned.1.call-start
  6.5 0.7 convert_element_type.7
  7.2 0.1 broadcast_in_dim.14
  7.3 0.1 reshape.21
  7.4 1.2 copy.21
  8.5 0.0 copy-start.1
  8.6 0.0 copy-start
  8.6 3.4 %collective-permute-start = (f32[384,256]{0,1:T(8,128)S(1)}, f32[384,256]{0,1:T(8,128)S(1)}, u32[]{:S(2)}, u32[]{:S(2)}) collective-permute-start(f32[384,256]{0,1:T(8,128)S(1)} %bitcast_multiply_fusion), channel_id=1, source_target_pairs={{0,64},{64,0},{1,65},{65,1},{2,66},{66,2},{3,67},{67,3},{4,68},{68... | collective-permute-start | bytes 1179656 | tf_op jit(solution)/shard_map/ppermute | solution.py:15
  12.0 9.5 %collective-permute-done = f32[384,256]{0,1:T(8,128)S(1)} collective-permute-done((f32[384,256]{0,1:T(8,128)S(1)}, f32[384,256]{0,1:T(8,128)S(1)}, u32[]{:S(2)}, u32[]{:S(2)}) %collective-permute-start) | collective-permute-done | bytes 393248 | tf_op jit(solution)/shard_map/ppermute | solution.py:15
  21.5 0.9 pad_maximum_fusion
  22.4 0.0 all-gather.2.cloned.1.call-update
  22.5 0.0 copy-done.1
  22.5 0.1 copy.19
  22.6 0.1 broadcast_in_dim.12
  22.6 0.1 reshape.19
  22.7 0.0 copy-done
  22.7 0.1 copy.20
  22.9 18.0 %all_gather.6 = f32[512,384]{0,1:T(8,128)S(1)} all-gather(f32[128,384]{0,1:T(8,128)S(1)} %bitcast_multiply_fusion.1), channel_id=1, replica_groups=mesh['h'=4,'l'=2,'c'=2,'x'=4,'z'=8] {'h'}, dimensions={0}, use_global_device_ids=true | all-gather | bytes 983040 | tf_op jit(solution)/shard_map/all_gather | solution.py:17
  40.9 3.8 %all-gather.2.cloned.1.call-done = f32[768,512]{0,1:T(8,128)} async-done(((f32[768,256]{0,1:T(8,128)}), f32[768,512]{0,1:T(8,128)}) %all-gather.2.cloned.1.call-update) | async-done | bytes 1572880 | tf_op jit(solution)/shard_map/all_gather | solution.py:19
  44.7 1.5 %slice_select_fusion.1 = (f32[384,512]{0,1:T(8,128)S(1)}, f32[384,512]{0,1:T(8,128)S(1)}) fusion(f32[768,512]{0,1:T(8,128)} %all-gather.2.cloned.1.call-done, pred[]{:T(512)S(6)} %eq.3), kind=kLoop, calls=%fused_computation.6 | loop fusion | flops 393216 | bytes 3145729 | tf_op jit(solution)/shard_map/jit(_where)/select_n | solution.py:24
  46.2 2.8 %fusion = f32[512,1024]{1,0:T(8,128)S(1)} fusion(f32[512,384]{0,1:T(8,128)S(1)} %all_gather.6, f32[384,512]{0,1:T(8,128)S(1)} %get-tuple-element.6, f32[384,512]{0,1:T(8,128)S(1)} %get-tuple-element.5), kind=kOutput, calls=%fused_computation | convolution fusion | flops 1208352768 | bytes 4456448 | tf_op jit(solution)/shard_map/dot_general | solution.py:25
  49.0 30.8 %all_to_all.14 = f32[4,128,1024]{2,1,0:T(8,128)S(1)} all-to-all(f32[4,128,1024]{2,1,0:T(8,128)S(1)} %bitcast.13), channel_id=1, replica_groups=mesh['h'=4,'l'=2,'c'=2,'x'=4,'z'=8] {'x'}, dimensions={0} | all-to-all | bytes 4194304 | tf_op jit(solution)/shard_map/all_to_all | solution.py:29
  79.8 0.2 reduce_sum.18
  80.0 0.2 copy.22
  80.2 0.2 copy.23
  80.4 24.0 %all_to_all.15 = f32[8,128,128]{2,1,0:T(8,128)S(1)} all-to-all(f32[8,128,128]{2,1,0:T(8,128)S(1)} %copy.23), channel_id=1, replica_groups=mesh['h'=4,'l'=2,'c'=2,'x'=4,'z'=8] {'z'}, dimensions={0} | all-to-all | bytes 1048576 | tf_op jit(solution)/shard_map/all_to_all | solution.py:33
  104.5 2.0 %collective-permute-start.1 = (f32[128,128]{1,0:T(8,128)S(1)}, f32[128,128]{1,0:T(8,128)S(1)}, u32[]{:S(2)}, u32[]{:S(2)}) collective-permute-start(f32[128,128]{1,0:T(8,128)S(1)} %reduce_sum.19), channel_id=1, source_target_pairs={{0,0},{8,128},{16,256},{24,384},{128,8},{136,136},{144,264},{152,3... | collective-permute-start | bytes 196616 | tf_op jit(solution)/shard_map/ppermute | solution.py:36
  106.5 10.4 %collective-permute-done.1 = f32[128,128]{1,0:T(8,128)S(1)} collective-permute-done((f32[128,128]{1,0:T(8,128)S(1)}, f32[128,128]{1,0:T(8,128)S(1)}, u32[]{:S(2)}, u32[]{:S(2)}) %collective-permute-start.1) | collective-permute-done | bytes 65568 | tf_op jit(solution)/shard_map/ppermute | solution.py:36
  117.0 0.6 copy.25
  (4 shorter events, 0.1 us)
Async XLA Ops:
  6.5 38.2 %all-gather.2.cloned.1.call-start = ((), (), s32[]{:S(2)}) async-start(), calls=%async_computation.2 | async-start | bytes 2359296 | tf_op jit(solution)/shard_map/all_gather | solution.py:19
  8.5 13.9 %copy-start.1 = (s32[2,6]{1,0:T(2,128)S(1)}, s32[2,6]{1,0:T(2,128)}, u32[]{:S(2)}) copy-start(s32[2,6]{1,0:T(2,128)} %param.6) | copy-start | bytes 148
  8.6 14.2 %copy-start = (f32[128,384]{1,0:T(8,128)S(1)}, f32[128,384]{1,0:T(8,128)}, u32[]{:S(2)}) copy-start(f32[128,384]{1,0:T(8,128)} %param.4) | copy-start | bytes 589828
  8.6 12.9 %collective-permute-start = (f32[384,256]{0,1:T(8,128)S(1)}, f32[384,256]{0,1:T(8,128)S(1)}, u32[]{:S(2)}, u32[]{:S(2)}) collective-permute-start(f32[384,256]{0,1:T(8,128)S(1)} %bitcast_multiply_fusion), channel_id=1, source_target_pairs={{0,64},{64,0},{1,65},{65,1},{2,66},{66,2},{3,67},{67,3},{4,68},{68... | collective-permute-start | bytes 1179656 | tf_op jit(solution)/shard_map/ppermute | solution.py:15
  104.5 12.5 %collective-permute-start.1 = (f32[128,128]{1,0:T(8,128)S(1)}, f32[128,128]{1,0:T(8,128)S(1)}, u32[]{:S(2)}, u32[]{:S(2)}) collective-permute-start(f32[128,128]{1,0:T(8,128)S(1)} %reduce_sum.19), channel_id=1, source_target_pairs={{0,0},{8,128},{16,256},{24,384},{128,8},{136,136},{144,264},{152,3... | collective-permute-start | bytes 196616 | tf_op jit(solution)/shard_map/ppermute | solution.py:36
Sparse Core Ops, SparseCore 0:
  22.6 22.1 all-gather.1
